TPU v7x, 128 devices: a whole 4x4x4 slice. The times are simulated.
128 devices in a mesh: gr: 8 (over y_hi, z), gc: 16 (over y_lo, x, core).
Axes of the slice: x: 4, y: 4 (y_hi: 2, y_lo: 2; y = y_hi * 2 + y_lo), z: 4, core: 2. Of those that a mesh axis runs over, the one named last changes fastest.
Arguments:
- student: bfloat16 [16384, 1024], P(('gr', 'gc')), may hold values from -500 to 500
- teacher: bfloat16 [16384, 1024], P(('gr', 'gc')), may hold values from -500 to 500
Outputs:
- student_grad: float32 [16384, 1024], P(('gr', 'gc'))
All inputs are finite; a program needn't handle non-finite values.
Results may differ from a plain program's by a relative error of at most 0.0085.
Values may be sent and summed in bfloat16 or wider, within the bound.
A program may use at most 64 MiB of HBM per device.

v0:
```python
import jax
import jax.numpy as jnp
from jax import lax
from jax.sharding import PartitionSpec as P

D = 1024


def unit_rows(embedded):
    values = embedded.astype(jnp.float32)
    inverse_rms = lax.rsqrt(jnp.mean(values * values, axis=-1, keepdims=True) + 1e-06)
    unit = (values * inverse_rms * D ** (-0.5)).astype(jnp.bfloat16)
    return (unit, inverse_rms)


def mismatch_of(piece_s, piece_t, other_s, other_t):
    sim_student = lax.dot_general(
        piece_s, other_s, (((1,), (1,)), ((), ())), preferred_element_type=jnp.float32
    )
    sim_teacher = lax.dot_general(
        piece_t, other_t, (((1,), (1,)), ((), ())), preferred_element_type=jnp.float32
    )
    stretch = 0.5 * D**0.5
    return jnp.tanh(stretch * (sim_student - sim_teacher)).astype(jnp.bfloat16)


def local(student, teacher):
    unit_s, inv_s = unit_rows(student)
    unit_t, inv_t = unit_rows(teacher)
    column_s, column_t = (
        lax.all_gather(unit_s, "gr", axis=0, tiled=True),
        lax.all_gather(unit_t, "gr", axis=0, tiled=True),
    )
    row_s, row_t = (
        lax.all_gather(unit_s, "gc", axis=0, tiled=True),
        lax.all_gather(unit_t, "gc", axis=0, tiled=True),
    )
    mismatch = mismatch_of(row_s, row_t, column_s, column_t)
    pull = lax.psum_scatter(
        jnp.dot(mismatch, column_s, preferred_element_type=jnp.float32),
        "gc",
        scatter_dimension=0,
        tiled=True,
    )
    unit_float = unit_s.astype(jnp.float32)
    radial = jnp.sum(unit_float * pull, axis=-1, keepdims=True)
    total_rows = unit_s.shape[0] * lax.axis_size("gr") * lax.axis_size("gc")
    factor = 12.0 * (D / total_rows) ** 0.5
    return factor * inv_s * (pull - radial * unit_float)


def solution(mesh):
    in_specs = (P(("gr", "gc"), None), P(("gr", "gc"), None))
    out_specs = P(("gr", "gc"), None)
    return jax.shard_map(local, mesh=mesh, in_specs=in_specs, out_specs=out_specs, check_vma=False)
```

profile of v0, /device:TPU:1, one launch (start us, length us, event | category | flops | bytes accessed | tf_op | source)
XLA Modules:
  0.0 292.6 jit_solution(11600875809418182227)
XLA Ops:
  6.5 0.0 all-gather.7.cloned.1.call-start
  6.5 1.1 fusion.4
  7.6 1.8 fusion.6
  9.4 0.0 all-gather.7.cloned.1.call-update
  9.4 0.0 all-gather.5.cloned.1.call-start
  9.5 0.7 all-gather.5.cloned.1.call-update
  10.2 0.0 all-gather.11.cloned.1.call-start
  10.2 1.1 fusion.7
  11.3 1.8 fusion.9
  13.1 0.0 all-gather.11.cloned.1.call-update
  13.2 0.0 all-gather.9.cloned.1.call-start
  13.2 0.5 all-gather.9.cloned.1.call-update
  13.7 0.0 reduce-scatter.2.cloned.1.call-start
  13.8 52.9 %all-gather.7.cloned.1.call-done = bf16[1024,1024]{1,0:T(8,128)(2,1)} async-done(((bf16[128,1024]{1,0:T(8,128)(2,1)}), bf16[1024,1024]{1,0:T(8,128)(2,1)}) %all-gather.7.cloned.1.call-update) | async-done | bytes 2097168 | tf_op jit(solution)/shard_map/all_gather | solution.py:31
  66.7 0.0 copy-start.1
  66.7 37.6 %all-gather.5.cloned.1.call-done = bf16[2048,1024]{1,0:T(8,128)(2,1)} async-done(((bf16[128,1024]{1,0:T(8,128)(2,1)}), bf16[2048,1024]{1,0:T(8,128)(2,1)}) %all-gather.5.cloned.1.call-update) | async-done | bytes 4194320 | tf_op jit(solution)/shard_map/all_gather | solution.py:35
  104.3 10.7 %fusion.14 = f32[2048,1024]{1,0:T(8,128)} fusion(bf16[2048,1024]{1,0:T(8,128)(2,1)} %all-gather.5.cloned.1.call-done, bf16[1024,1024]{1,0:T(8,128)(2,1)} %all-gather.7.cloned.1.call-done), kind=kOutput, calls=%fused_computation.23 | convolution fusion | flops 4294967296 | bytes 14680064 | tf_op jit(solution)/shard_map/dot_general | solution.py:17
  115.0 45.2 %all-gather.11.cloned.1.call-done = bf16[1024,1024]{1,0:T(8,128)(2,1)} async-done(((bf16[128,1024]{1,0:T(8,128)(2,1)}), bf16[1024,1024]{1,0:T(8,128)(2,1)}) %all-gather.11.cloned.1.call-update) | async-done | bytes 2097168 | tf_op jit(solution)/shard_map/all_gather | solution.py:32
  160.1 37.4 %all-gather.9.cloned.1.call-done = bf16[2048,1024]{1,0:T(8,128)(2,1)} async-done(((bf16[128,1024]{1,0:T(8,128)(2,1)}), bf16[2048,1024]{1,0:T(8,128)(2,1)}) %all-gather.9.cloned.1.call-update) | async-done | bytes 4194320 | tf_op jit(solution)/shard_map/all_gather | solution.py:36
  197.6 0.0 copy-done.1
  197.6 14.5 %fusion = f32[2048,1024]{1,0:T(8,128)} fusion(bf16[1024,1024]{1,0:T(8,128)(2,1)S(1)} %copy-done.1, f32[2048,1024]{1,0:T(8,128)} %fusion.14, bf16[2048,1024]{1,0:T(8,128)(2,1)} %all-gather.9.cloned.1.call-done, bf16[1024,1024]{1,0:T(8,128)(2,1)} %all-gather.11.cloned.1.call-done), kind=kOutput, calls=%fused_computation.1 | convolution fusion | flops 8596226048 | bytes 25165824 | tf_op jit(solution)/shard_map/dot_general | solution.py:40
  212.1 0.0 copy-start
  212.1 0.0 reduce-scatter.2.cloned.1.call-update
  212.1 70.6 %reduce-scatter.2.cloned.1.call-done = f32[128,1024]{1,0:T(8,128)} async-done(((f32[2048,1024]{1,0:T(8,128)}), f32[128,1024]{1,0:T(8,128)}) %reduce-scatter.2.cloned.1.call-update) | async-done | bytes 524304 | tf_op jit(solution)/shard_map/reduce_scatter | solution.py:39
  282.7 0.0 copy-done
  282.7 1.3 fusion.10
  284.0 2.1 fusion.12
  (2 shorter events, 0.0 us)
Async XLA Ops:
  6.5 60.2 %all-gather.7.cloned.1.call-start = ((), (), s32[]{:S(2)}) async-start(), calls=%async_computation.2 | async-start | bytes 2359296 | tf_op jit(solution)/shard_map/all_gather | solution.py:31
  9.4 94.9 %all-gather.5.cloned.1.call-start = ((), (), s32[]{:S(2)}) async-start(), calls=%async_computation.1 | async-start | bytes 4456448 | tf_op jit(solution)/shard_map/all_gather | solution.py:35
  10.2 149.9 %all-gather.11.cloned.1.call-start = ((), (), s32[]{:S(2)}) async-start(), calls=%async_computation.4 | async-start | bytes 2359296 | tf_op jit(solution)/shard_map/all_gather | solution.py:32
  13.2 184.4 %all-gather.9.cloned.1.call-start = ((), (), s32[]{:S(2)}) async-start(), calls=%async_computation.3 | async-start | bytes 4456448 | tf_op jit(solution)/shard_map/all_gather | solution.py:36
  13.7 268.9 %reduce-scatter.2.cloned.1.call-start = ((), (), s32[]{:S(2)}) async-start(), calls=%async_computation.5 | async-start | bytes 8912896 | tf_op jit(solution)/shard_map/reduce_scatter | solution.py:39
  66.7 130.8 %copy-start.1 = (bf16[1024,1024]{1,0:T(8,128)(2,1)S(1)}, bf16[1024,1024]{1,0:T(8,128)(2,1)}, u32[]{:S(2)}) copy-start(bf16[1024,1024]{1,0:T(8,128)(2,1)} %all-gather.7.cloned.1.call-done) | copy-start | bytes 6291460
  212.1 70.6 %copy-start = (bf16[128,1024]{1,0:T(8,128)(2,1)S(1)}, bf16[128,1024]{1,0:T(8,128)(2,1)}, u32[]{:S(2)}) copy-start(bf16[128,1024]{1,0:T(8,128)(2,1)} %param.2) | copy-start | bytes 786436
Sparse Core Ops, SparseCore 0:
  9.7 56.9 all-gather.6
  68.4 35.8 all-gather.4
  106.7 53.4 all-gather.10
  161.7 35.8 all-gather.8
  212.2 70.4 reduce-scatter.1
where the time goes:
time: 296 us; the launch traced here: 293 us
  waiting for transfers between devices  245 us (83%)
  matrix products  25.2 us (9%)
  between operations  13.1 us (4%)
  other arithmetic  9.12 us (3%)
    reduce_scatter x1, waiting for transfers between devices, local(): lax.psum_scatter(jnp.dot(mismatch, column_s, preferred_element_type=jnp.f...  70.6 us
    all_gather x1, waiting for transfers between devices, local(): lax.all_gather(unit_s, 'gr', axis=0, tiled=True)  52.9 us
    all_gather x1, waiting for transfers between devices, local(): lax.all_gather(unit_t, 'gr', axis=0, tiled=True)  45.2 us
    all_gather x1, waiting for transfers between devices, local(): lax.all_gather(unit_s, 'gc', axis=0, tiled=True)  37.6 us
    all_gather x1, waiting for transfers between devices, local(): lax.all_gather(unit_t, 'gc', axis=0, tiled=True)  37.4 us
    dot_general x1, matrix products, local(): jnp.dot(mismatch, column_s, preferred_element_type=jnp.float32)  14.5 us
    dot_general x1, matrix products, mismatch_of(): lax.dot_general(piece_s, other_s, (((1,), (1,)), ((), ())), preferred_ele...  10.7 us
  transfers between devices with their start and end apart: 5, of which 5 were waited for; matrix products, arithmetic and copies ran while one was open for 5% of the time, Pallas kernels for 0%

commit v1 on v0

v1 whole, which is shorter than its diff:
```python
import jax
import jax.numpy as jnp
from jax import lax
from jax.experimental import pallas as pl
from jax.experimental.pallas import tpu as pltpu
from jax.sharding import PartitionSpec as P

D = 1024
F32 = jnp.float32
BF16 = jnp.bfloat16
MESH = pl.DeviceIdType.MESH

HELD = (30, 0, 48, 100, 32, 124, 93, 29, 22, 84, 21, 85, 4, 26, 20, 94)
PARENT = ((13, 2, 4, 14, 3, 2, 7, 15, 10, 11, 11, -1, 14, 8, 9, 0), (13, 2, 4, 9, 3, 2, 7, 0, 11, 11, 11, -1, 9, 8, 9, 0), (13, 12, 1, 14, 2, 2, 7, 0, 10, 10, 11, -1, 14, 8, 9, 0), (13, 12, 1, 9, 2, 2, 0, 6, 10, 11, 11, -1, 9, 8, 9, 0))
SLOT = ((6, 7, 5, 3, 4, 9, 7, 7, 1, 2, -1, -1, 5, 5, 2, 6), (8, 8, 4, 2, 3, 8, 9, 9, 3, 1, -1, -1, 2, 7, 1, 8), (2, 5, 6, 6, 8, 7, 4, 4, 0, 3, -1, -1, 4, 1, 3, 2), (4, 2, 3, 1, 7, 6, 5, 5, 2, 0, -1, -1, 1, 3, 0, 4))
TASKS = ((4, 4), (5, 1), (4, 1), (6, 5), (6, 4), (6, 1), (7, 6), (7, 4), (5, 0), (4, 0), (7, 2), (6, 3), (6, 2), (5, 2), (4, 2), (3, 2), (3, 1), (3, 0), (2, 1), (2, 0))
N = len(HELD)
ROWS = 128
PIECES = len(PARENT)
PIECE = ROWS // PIECES
OWN = PARENT[0].index(-1)
STAGES = 1 + max(map(max, SLOT))
PER_STAGE = 3


def parts(offset):
    return tuple((offset >> s) & 3 for s in (0, 2, 4)) + (offset >> 6,)


def minus(a, b):
    sizes = (4, 4, 4, 2)
    return tuple((p - q) % n for p, q, n in zip(parts(a), parts(b), sizes))


def same_chip(h, j):
    return minus(HELD[PARENT[h][j]], HELD[j])[:3] == (0, 0, 0)


def stages():
    out = [[] for _ in range(STAGES + 1)]
    for h in range(PIECES):
        for j in range(N):
            if j != OWN:
                near = same_chip(h, j)
                out[SLOT[h][j] + near].append((h, j, PARENT[h][j], near))
    for t, sends in enumerate(out):
        fresh = {(h, j) for h, j, _, near in sends if near}
        sends.sort(key=lambda s: (not s[3], (s[0], s[2]) in fresh))
    return [[s[:3] for s in sends] for sends in out]


def weights():
    done, out = set(), []
    for g, h in TASKS:
        quad = [[0.0, 0.0], [0.0, 0.0]]
        for p in range(2):
            for q in range(2):
                a, b = HELD[2 * g + p], HELD[2 * h + q]
                there, back = minus(a, b), minus(b, a)
                if min(there, back) in done:
                    continue
                if g == h and p < q:
                    continue
                done.add(min(there, back))
                weight = 0.5 if there == back and any(there) else 1.0
                quad[p][q] = weight
                if g == h:
                    quad[q][p] = weight
        out.append(quad)
    assert len(done) == 72
    return out


def kernel(student_ref, teacher_ref, out_ref, held, pull, sent, come, g_send, g_recv, r_send, r_recv):
    gr, gc = lax.axis_index("gr"), lax.axis_index("gc")
    place = (lax.rem(gc // 2, 4), (gr // 4) * 2 + gc // 8, lax.rem(gr, 4), lax.rem(gc, 2))

    def device(step):
        x, y, z, c = (lax.rem(p + s, n) for p, s, n in zip(place, step, (4, 4, 4, 2)))
        return ((y // 2) * 4 + z, lax.rem(y, 2) * 8 + x * 2 + c)

    plan = stages()
    edges = [e for sends in plan for e in sends]
    steps = set()
    for h, j, i in edges:
        steps |= {minus(HELD[i], HELD[j]), minus(HELD[j], HELD[i])}
    target = {step: device(step) for step in sorted(steps)}

    barrier = pltpu.get_barrier_semaphore()
    for step in target:
        pl.semaphore_signal(barrier, inc=1, device_id=target[step], device_id_type=MESH)

    def unit(ref, rows):
        values = ref[rows, :].astype(F32)
        inverse = lax.rsqrt(jnp.mean(values * values, axis=-1, keepdims=True) + 1e-06)
        return (values * inverse * D ** (-0.5)).astype(BF16), inverse

    def rows_of(h):
        return pl.ds(h * PIECE, PIECE)

    for h in range(PIECES):
        held[OWN, rows_of(h), 0:D] = unit(student_ref, rows_of(h))[0]
        held[OWN, rows_of(h), D : 2 * D] = unit(teacher_ref, rows_of(h))[0]
    pl.semaphore_wait(barrier, len(target))

    arrived = {(h, OWN) for h in range(PIECES)}
    gathers, returns = {}, {}

    def await_piece(h, j):
        if (h, j) not in arrived:
            gathers[h, j].wait_recv()
            arrived.add((h, j))

    tasks = list(zip(TASKS, weights()))
    fresh = set(range(N // 2))

    def add(g, value):
        value = value.reshape(2, ROWS, D)
        if g in fresh:
            pull[2 * g : 2 * g + 2] = value
            fresh.discard(g)
        else:
            pull[2 * g : 2 * g + 2] += value

    def dot(a, b, dims):
        return lax.dot_general(a, b, (dims, ((), ())), preferred_element_type=F32)

    def run(task):
        (g, h), quad = task
        for b in (2 * g, 2 * g + 1, 2 * h, 2 * h + 1):
            for piece in range(PIECES):
                await_piece(piece, b)
        s_g = held[2 * g : 2 * g + 2, :, 0:D].reshape(2 * ROWS, D)
        s_h = held[2 * h : 2 * h + 2, :, 0:D].reshape(2 * ROWS, D)
        t_g = held[2 * g : 2 * g + 2, :, D : 2 * D].reshape(2 * ROWS, D)
        t_h = held[2 * h : 2 * h + 2, :, D : 2 * D].reshape(2 * ROWS, D)
        gap = dot(s_g, s_h, ((1,), (1,))) - dot(t_g, t_h, ((1,), (1,)))
        lines = []
        for p in range(2):
            line = []
            for q in range(2):
                if quad[p][q] == 0.0:
                    line.append(jnp.zeros((ROWS, ROWS), BF16))
                    continue
                part = gap[p * ROWS : (p + 1) * ROWS, q * ROWS : (q + 1) * ROWS]
                value = jnp.tanh(0.5 * D**0.5 * part).astype(BF16)
                line.append(value if quad[p][q] == 1.0 else value * jnp.asarray(quad[p][q], BF16))
            lines.append(jnp.concatenate(line, axis=1))
        mismatch = jnp.concatenate(lines, axis=0)
        add(g, dot(mismatch, s_h, ((1,), (0,))))
        if g != h:
            add(h, dot(mismatch, s_g, ((0,), (0,))))


    ready = [0] * (N // 2)
    for h, j, _ in edges:
        ready[j // 2] = max(ready[j // 2], SLOT[h][j] + 1 + same_chip(h, j))

    for t, sends in enumerate(plan):
        for h, j, i in sends:
            await_piece(h, i)
            gathers[h, j] = pltpu.make_async_remote_copy(
                src_ref=held.at[i, rows_of(h), :],
                dst_ref=held.at[j, rows_of(h), :],
                send_sem=g_send.at[h, j],
                recv_sem=g_recv.at[h, j],
                device_id=target[minus(HELD[i], HELD[j])],
                device_id_type=MESH,
            )
            gathers[h, j].start()
        for task in [k for k in tasks if max(ready[b] for b in k[0]) <= t][:PER_STAGE]:
            run(task)
            tasks.remove(task)

    def total(h, j):
        for task in [k for k in tasks if j // 2 in k[0]]:
            run(task)
            tasks.remove(task)
        value = pull[j, rows_of(h), :]
        for child in range(N):
            if PARENT[h][child] == j:
                returns[h, child].wait_recv()
                value += come[child, rows_of(h), :].astype(F32)
        return value

    for h, j, i in reversed(edges):
        sent[j, rows_of(h), :] = total(h, j).astype(BF16)
        returns[h, j] = pltpu.make_async_remote_copy(
            src_ref=sent.at[j, rows_of(h), :],
            dst_ref=come.at[j, rows_of(h), :],
            send_sem=r_send.at[h, j],
            recv_sem=r_recv.at[h, j],
            device_id=target[minus(HELD[j], HELD[i])],
            device_id_type=MESH,
        )
        returns[h, j].start()

    scale = 12.0 * (D / (ROWS * 128)) ** 0.5
    for h in range(PIECES):
        value = total(h, OWN)
        unit_float = held[OWN, rows_of(h), 0:D].astype(F32)
        inverse = unit(student_ref, rows_of(h))[1]
        radial = jnp.sum(unit_float * value, axis=-1, keepdims=True)
        out_ref[rows_of(h), :] = scale * inverse * (value - radial * unit_float)
    for h, j, _ in edges:
        await_piece(h, j)
        gathers[h, j].wait_send()
        returns[h, j].wait_send()


def local(student, teacher):
    vmem = pl.BlockSpec(memory_space=pltpu.VMEM)
    sems = pltpu.SemaphoreType.DMA((PIECES, N))
    return pl.pallas_call(
        kernel,
        out_shape=jax.ShapeDtypeStruct((ROWS, D), F32),
        in_specs=[vmem, vmem],
        out_specs=vmem,
        scratch_shapes=[
            pltpu.VMEM((N, ROWS, 2 * D), BF16),
            pltpu.VMEM((N, ROWS, D), F32),
            pltpu.VMEM((N, ROWS, D), BF16),
            pltpu.VMEM((N, ROWS, D), BF16),
            sems,
            sems,
            sems,
            sems,
        ],
        compiler_params=pltpu.CompilerParams(
            collective_id=0, has_side_effects=True, vmem_limit_bytes=56 * 2**20
        ),
        name="relational_grad",
    )(student, teacher)


def solution(mesh):
    spec = P(("gr", "gc"), None)
    return jax.shard_map(local, mesh=mesh, in_specs=(spec, spec), out_specs=spec, check_vma=False)
```

time: 296 us -> 109 us (0.37); the launches traced: 293 us -> 109 us
  waiting for transfers between devices: 245 us -> 0 us
  Pallas kernels: 0 us -> 107 us
  matrix products: 25.2 us -> 0 us
  between operations: 13.1 us -> 0.01 us
  other arithmetic: 9.12 us -> 0 us
    all_gather x4 -> x0, waiting for transfers between devices: 173 us -> none  [the longest x1 52.9 us: local(): lax.all_gather(unit_s, 'gr', axis=0, tiled=True)]
    pallas_call x0 -> x1, Pallas kernels: none -> 107 us  [local(): pl.pallas_call(kernel, out_shape=jax.ShapeDtypeStruct((ROWS, D), F32), in...]
    reduce_scatter x1 -> x0, waiting for transfers between devices: 70.6 us -> none  [local(): lax.psum_scatter(jnp.dot(mismatch, column_s, preferred_element_type=jnp.f...]
    dot_general x2 -> x0, matrix products: 25.2 us -> none  [the longest x1 14.5 us: local(): jnp.dot(mismatch, column_s, preferred_element_type=jnp.float32)]
    convert_element_type x2 -> x0, other arithmetic: 3.59 us -> none  [unit_rows(): unit = (values * inverse_rms * D ** (-0.5)).astype(jnp.bfloat16)]
    reduce_sum x3 -> x0, other arithmetic: 3.44 us -> none  [the longest x2 2.17 us: unit_rows(): jnp.mean(values * values, axis=-1, keepdims=True) + 1e-06]
  transfers between devices with their start and end apart: 5 -> 0, of which waited for: 5 -> 0; matrix products, arithmetic and copies ran while one was open for 5% -> 0% of each run, Pallas kernels for 0% -> 0%
where the time goes in v1:
time: 109 us
  Pallas kernels  107 us (98%)
  local copies, waits for them, and re-layouts  1.89 us (2%)
    pallas_call x1, Pallas kernels, local(): pl.pallas_call(kernel, out_shape=jax.ShapeDtypeStruct((ROWS, D), F32), in...  107 us

profile of v1, /device:TPU:1, one launch (start us, length us, event | category | flops | bytes accessed | tf_op | source)
XLA Modules:
  0.0 109.0 jit_solution(3949828237232138203)
XLA Ops:
  0.0 107.1 %relational_grad.1 = f32[128,1024]{1,0:T(8,128)} custom-call(bf16[128,1024]{1,0:T(8,128)(2,1)} %student_ref.1, bf16[128,1024]{1,0:T(8,128)(2,1)} %teacher_ref.1), custom_call_target="tpu_custom_call" | custom-call | tf_op jit(solution)/shard_map/relational_grad/pallas_call | solution.py:214
  107.1 1.9 %copy.4 = f32[128,1024]{1,0:T(8,128)} copy(f32[128,1024]{1,0:T(8,128)} %relational_grad.1) | data formatting | bytes 1048576

commit v2 on v1

--- a/solution.py
+++ b/solution.py
@@ -10,17 +10,17 @@
 BF16 = jnp.bfloat16
 MESH = pl.DeviceIdType.MESH
 
-HELD = (30, 0, 48, 100, 32, 124, 93, 29, 22, 84, 21, 85, 4, 26, 20, 94)
-PARENT = ((13, 2, 4, 14, 3, 2, 7, 15, 10, 11, 11, -1, 14, 8, 9, 0), (13, 2, 4, 9, 3, 2, 7, 0, 11, 11, 11, -1, 9, 8, 9, 0), (13, 12, 1, 14, 2, 2, 7, 0, 10, 10, 11, -1, 14, 8, 9, 0), (13, 12, 1, 9, 2, 2, 0, 6, 10, 11, 11, -1, 9, 8, 9, 0))
-SLOT = ((6, 7, 5, 3, 4, 9, 7, 7, 1, 2, -1, -1, 5, 5, 2, 6), (8, 8, 4, 2, 3, 8, 9, 9, 3, 1, -1, -1, 2, 7, 1, 8), (2, 5, 6, 6, 8, 7, 4, 4, 0, 3, -1, -1, 4, 1, 3, 2), (4, 2, 3, 1, 7, 6, 5, 5, 2, 0, -1, -1, 1, 3, 0, 4))
-TASKS = ((4, 4), (5, 1), (4, 1), (6, 5), (6, 4), (6, 1), (7, 6), (7, 4), (5, 0), (4, 0), (7, 2), (6, 3), (6, 2), (5, 2), (4, 2), (3, 2), (3, 1), (3, 0), (2, 1), (2, 0))
+HELD = (72, 76, 91, 89, 113, 125, 49, 126, 11, 24, 124, 62, 0, 64, 59, 123)
+STEPS = ((0, 6, 5), (5, 10, 5), (5, 11, 5), (2, 7, 5), (6, 10, 5), (7, 6, 5), (1, 10, 5), (2, 4, 5), (6, 11, 5), (1, 11, 5), (5, 6, 5), (7, 10, 5), (0, 4, 6), (5, 1, 10), (5, 7, 11), (3, 4, 5), (3, 7, 5), (4, 10, 5), (2, 11, 7), (6, 1, 10), (7, 4, 6), (1, 4, 5), (3, 10, 5), (7, 11, 5), (1, 1, 10), (2, 6, 4), (6, 7, 11), (5, 0, 1), (0, 10, 5), (0, 11, 5), (6, 4, 5), (1, 7, 11), (5, 4, 6), (7, 1, 10), (6, 0, 1), (2, 10, 5), (4, 7, 5), (5, 12, 1), (3, 6, 4), (3, 11, 7), (4, 1, 10), (1, 0, 1), (5, 9, 0), (1, 6, 4), (7, 7, 11), (3, 1, 10), (7, 0, 1), (7, 12, 1), (6, 8, 0), (6, 12, 1), (0, 7, 11), (6, 6, 4), (4, 0, 1), (1, 8, 0), (4, 4, 5), (2, 1, 10), (4, 11, 7), (5, 13, 12), (1, 9, 0), (5, 3, 9), (5, 2, 9), (5, 5), (7, 13, 12), (7, 8, 0), (6, 14, 8), (0, 1, 10), (3, 0, 1), (3, 13, 1), (6, 13, 12), (4, 8, 0), (1, 15, 8), (6, 9, 0), (2, 0, 1), (2, 12, 1), (1, 12, 1), (4, 6, 4), (5, 8, 2), (4, 9, 0), (1, 3, 9), (6, 15, 14), (3, 8, 0), (4, 12, 1), (3, 12, 13), (7, 14, 8), (0, 0, 1), (1, 14, 15), (2, 8, 0), (2, 9, 0), (0, 12, 1), (2, 13, 12), (1, 2, 9), (4, 15, 8), (3, 9, 0), (6, 3, 9), (5, 2), (1, 13, 12), (3, 14, 8), (7, 9, 0), (4, 3, 9), (7, 15, 14), (0, 8, 0), (4, 13, 12), (4, 2, 9), (2, 14, 8), (0, 9, 0), (2, 3, 9), (5, 15, 8), (4, 14, 15), (5, 3), (0, 13, 12), (2, 2, 9), (6, 2, 8), (3, 3, 9), (3, 15, 14), (5, 0), (3, 2, 9), (0, 15, 8), (0, 2, 8), (7, 3, 9), (2, 15, 14), (3, 0), (7, 2, 9), (0, 3, 9), (5, 14, 15), (2, 0), (6, 5), (0, 14, 15))
+LATE = ((6, 2), (6, 0), (6, 4), (5, 4), (4, 3), (4, 2), (4, 0), (7, 6), (7, 4), (7, 2), (7, 0), (7, 1), (5, 1), (3, 1), (2, 1))
+RETURNS = ((2, 14, 15), (2, 2, 8), (2, 3, 9), (2, 15, 8), (3, 14, 15), (3, 2, 9), (3, 3, 9), (3, 15, 8), (1, 14, 15), (0, 2, 8), (1, 2, 9), (1, 3, 9), (1, 15, 8), (0, 14, 15), (2, 8, 0), (2, 9, 0), (0, 3, 9), (0, 15, 8), (3, 8, 0), (3, 9, 0), (1, 8, 0), (1, 9, 0), (2, 13, 12), (2, 0, 1), (2, 12, 1), (0, 8, 0), (0, 9, 0), (3, 12, 13), (3, 0, 1), (3, 13, 1), (1, 13, 12), (1, 0, 1), (1, 12, 1), (0, 13, 12), (2, 1, 10), (0, 0, 1), (0, 12, 1), (3, 1, 10), (1, 1, 10), (0, 4, 6), (2, 11, 7), (0, 6, 5), (2, 7, 5), (2, 10, 5), (0, 1, 10), (1, 7, 11), (3, 6, 4), (1, 11, 5), (3, 4, 5), (3, 10, 5), (0, 11, 7), (1, 4, 6), (0, 7, 5), (1, 6, 5), (1, 10, 5), (2, 4, 6), (3, 11, 7), (0, 10, 5), (2, 6, 5), (3, 7, 5))
 N = len(HELD)
 ROWS = 128
-PIECES = len(PARENT)
-PIECE = ROWS // PIECES
-OWN = PARENT[0].index(-1)
-STAGES = 1 + max(map(max, SLOT))
-PER_STAGE = 3
+TASKS = tuple(s for s in STEPS if len(s) == 2) + LATE
+SENDS = tuple(s for s in STEPS if len(s) == 3)
+OWN = ({i for _, _, i in SENDS} - {j for _, j, _ in SENDS}).pop()
+PIECES = 1 + max(h for h, _, _ in SENDS)
+PARTS = 1 + max(h for h, _, _ in RETURNS)
 
 
 def parts(offset):
@@ -30,23 +30,6 @@
 def minus(a, b):
     sizes = (4, 4, 4, 2)
     return tuple((p - q) % n for p, q, n in zip(parts(a), parts(b), sizes))
-
-
-def same_chip(h, j):
-    return minus(HELD[PARENT[h][j]], HELD[j])[:3] == (0, 0, 0)
-
-
-def stages():
-    out = [[] for _ in range(STAGES + 1)]
-    for h in range(PIECES):
-        for j in range(N):
-            if j != OWN:
-                near = same_chip(h, j)
-                out[SLOT[h][j] + near].append((h, j, PARENT[h][j], near))
-    for t, sends in enumerate(out):
-        fresh = {(h, j) for h, j, _, near in sends if near}
-        sends.sort(key=lambda s: (not s[3], (s[0], s[2]) in fresh))
-    return [[s[:3] for s in sends] for sends in out]
 
 
 def weights():
@@ -79,10 +62,8 @@
         x, y, z, c = (lax.rem(p + s, n) for p, s, n in zip(place, step, (4, 4, 4, 2)))
         return ((y // 2) * 4 + z, lax.rem(y, 2) * 8 + x * 2 + c)
 
-    plan = stages()
-    edges = [e for sends in plan for e in sends]
     steps = set()
-    for h, j, i in edges:
+    for _, j, i in SENDS + RETURNS:
         steps |= {minus(HELD[i], HELD[j]), minus(HELD[j], HELD[i])}
     target = {step: device(step) for step in sorted(steps)}
 
@@ -96,7 +77,10 @@
         return (values * inverse * D ** (-0.5)).astype(BF16), inverse
 
     def rows_of(h):
-        return pl.ds(h * PIECE, PIECE)
+        return pl.ds(h * (ROWS // PIECES), ROWS // PIECES)
+
+    def part_of(h):
+        return pl.ds(h * (ROWS // PARTS), ROWS // PARTS)
 
     for h in range(PIECES):
         held[OWN, rows_of(h), 0:D] = unit(student_ref, rows_of(h))[0]
@@ -151,43 +135,38 @@
         if g != h:
             add(h, dot(mismatch, s_g, ((0,), (0,))))
 
-
-    ready = [0] * (N // 2)
-    for h, j, _ in edges:
-        ready[j // 2] = max(ready[j // 2], SLOT[h][j] + 1 + same_chip(h, j))
-
-    for t, sends in enumerate(plan):
-        for h, j, i in sends:
-            await_piece(h, i)
-            gathers[h, j] = pltpu.make_async_remote_copy(
-                src_ref=held.at[i, rows_of(h), :],
-                dst_ref=held.at[j, rows_of(h), :],
-                send_sem=g_send.at[h, j],
-                recv_sem=g_recv.at[h, j],
-                device_id=target[minus(HELD[i], HELD[j])],
-                device_id_type=MESH,
-            )
-            gathers[h, j].start()
-        for task in [k for k in tasks if max(ready[b] for b in k[0]) <= t][:PER_STAGE]:
-            run(task)
-            tasks.remove(task)
+    for step in STEPS:
+        if len(step) == 2:
+            run(tasks.pop(0))
+            continue
+        h, j, i = step
+        await_piece(h, i)
+        gathers[h, j] = pltpu.make_async_remote_copy(
+            src_ref=held.at[i, rows_of(h), :],
+            dst_ref=held.at[j, rows_of(h), :],
+            send_sem=g_send.at[h, j],
+            recv_sem=g_recv.at[h, j],
+            device_id=target[minus(HELD[i], HELD[j])],
+            device_id_type=MESH,
+        )
+        gathers[h, j].start()
 
     def total(h, j):
         for task in [k for k in tasks if j // 2 in k[0]]:
             run(task)
             tasks.remove(task)
-        value = pull[j, rows_of(h), :]
-        for child in range(N):
-            if PARENT[h][child] == j:
+        value = pull[j, part_of(h), :]
+        for part, child, parent in RETURNS:
+            if (part, parent) == (h, j):
                 returns[h, child].wait_recv()
-                value += come[child, rows_of(h), :].astype(F32)
+                value += come[child, part_of(h), :].astype(F32)
         return value
 
-    for h, j, i in reversed(edges):
-        sent[j, rows_of(h), :] = total(h, j).astype(BF16)
+    for h, j, i in RETURNS:
+        sent[j, part_of(h), :] = total(h, j).astype(BF16)
         returns[h, j] = pltpu.make_async_remote_copy(
-            src_ref=sent.at[j, rows_of(h), :],
-            dst_ref=come.at[j, rows_of(h), :],
+            src_ref=sent.at[j, part_of(h), :],
+            dst_ref=come.at[j, part_of(h), :],
             send_sem=r_send.at[h, j],
             recv_sem=r_recv.at[h, j],
             device_id=target[minus(HELD[j], HELD[i])],
@@ -196,21 +175,22 @@
         returns[h, j].start()
 
     scale = 12.0 * (D / (ROWS * 128)) ** 0.5
-    for h in range(PIECES):
+    for h in range(PARTS):
         value = total(h, OWN)
-        unit_float = held[OWN, rows_of(h), 0:D].astype(F32)
-        inverse = unit(student_ref, rows_of(h))[1]
+        unit_float = held[OWN, part_of(h), 0:D].astype(F32)
+        inverse = unit(student_ref, part_of(h))[1]
         radial = jnp.sum(unit_float * value, axis=-1, keepdims=True)
-        out_ref[rows_of(h), :] = scale * inverse * (value - radial * unit_float)
-    for h, j, _ in edges:
-        await_piece(h, j)
+        out_ref[part_of(h), :] = scale * inverse * (value - radial * unit_float)
+    for h, j, _ in SENDS:
         gathers[h, j].wait_send()
+    for h, j, _ in RETURNS:
         returns[h, j].wait_send()
 
 
 def local(student, teacher):
     vmem = pl.BlockSpec(memory_space=pltpu.VMEM)
-    sems = pltpu.SemaphoreType.DMA((PIECES, N))
+    g_sems = pltpu.SemaphoreType.DMA((PIECES, N))
+    r_sems = pltpu.SemaphoreType.DMA((PARTS, N))
     return pl.pallas_call(
         kernel,
         out_shape=jax.ShapeDtypeStruct((ROWS, D), F32),
@@ -221,10 +201,10 @@
             pltpu.VMEM((N, ROWS, D), F32),
             pltpu.VMEM((N, ROWS, D), BF16),
             pltpu.VMEM((N, ROWS, D), BF16),
-            sems,
-            sems,
-            sems,
-            sems,
+            g_sems,
+            g_sems,
+            r_sems,
+            r_sems,
         ],
         compiler_params=pltpu.CompilerParams(
             collective_id=0, has_side_effects=True, vmem_limit_bytes=56 * 2**20

time: 109 us -> 81.7 us (0.75)
  Pallas kernels: 107 us -> 79.6 us
    pallas_call x1, Pallas kernels: 107 us -> 79.6 us  [local(): pl.pallas_call(kernel, out_shape=jax.ShapeDtypeStruct((ROWS, D), F32), in...]
where the time goes in v2:
time: 81.7 us; the launch traced here: 81.5 us
  Pallas kernels  79.6 us (97%)
  local copies, waits for them, and re-layouts  1.89 us (2%)
    pallas_call x1, Pallas kernels, local(): pl.pallas_call(kernel, out_shape=jax.ShapeDtypeStruct((ROWS, D), F32), in...  79.6 us
    unnamed x1, local copies, waits for them, and re-layouts  1.89 us

profile of v2, /device:TPU:1, one launch (start us, length us, event | category | flops | bytes accessed | tf_op | source)
XLA Modules:
  0.0 81.5 jit_solution(13824767385333690541)
XLA Ops:
  0.0 79.6 %relational_grad.1 = f32[128,1024]{1,0:T(8,128)} custom-call(bf16[128,1024]{1,0:T(8,128)(2,1)} %student_ref.1, bf16[128,1024]{1,0:T(8,128)(2,1)} %teacher_ref.1), custom_call_target="tpu_custom_call" | custom-call | tf_op jit(solution)/shard_map/relational_grad/pallas_call | solution.py:194
  79.7 1.9 %copy.4 = f32[128,1024]{1,0:T(8,128)} copy(f32[128,1024]{1,0:T(8,128)} %relational_grad.1) | data formatting | bytes 1048576

commit v3 on v2

--- a/solution.py
+++ b/solution.py
@@ -10,10 +10,10 @@
 BF16 = jnp.bfloat16
 MESH = pl.DeviceIdType.MESH
 
-HELD = (72, 76, 91, 89, 113, 125, 49, 126, 11, 24, 124, 62, 0, 64, 59, 123)
-STEPS = ((0, 6, 5), (5, 10, 5), (5, 11, 5), (2, 7, 5), (6, 10, 5), (7, 6, 5), (1, 10, 5), (2, 4, 5), (6, 11, 5), (1, 11, 5), (5, 6, 5), (7, 10, 5), (0, 4, 6), (5, 1, 10), (5, 7, 11), (3, 4, 5), (3, 7, 5), (4, 10, 5), (2, 11, 7), (6, 1, 10), (7, 4, 6), (1, 4, 5), (3, 10, 5), (7, 11, 5), (1, 1, 10), (2, 6, 4), (6, 7, 11), (5, 0, 1), (0, 10, 5), (0, 11, 5), (6, 4, 5), (1, 7, 11), (5, 4, 6), (7, 1, 10), (6, 0, 1), (2, 10, 5), (4, 7, 5), (5, 12, 1), (3, 6, 4), (3, 11, 7), (4, 1, 10), (1, 0, 1), (5, 9, 0), (1, 6, 4), (7, 7, 11), (3, 1, 10), (7, 0, 1), (7, 12, 1), (6, 8, 0), (6, 12, 1), (0, 7, 11), (6, 6, 4), (4, 0, 1), (1, 8, 0), (4, 4, 5), (2, 1, 10), (4, 11, 7), (5, 13, 12), (1, 9, 0), (5, 3, 9), (5, 2, 9), (5, 5), (7, 13, 12), (7, 8, 0), (6, 14, 8), (0, 1, 10), (3, 0, 1), (3, 13, 1), (6, 13, 12), (4, 8, 0), (1, 15, 8), (6, 9, 0), (2, 0, 1), (2, 12, 1), (1, 12, 1), (4, 6, 4), (5, 8, 2), (4, 9, 0), (1, 3, 9), (6, 15, 14), (3, 8, 0), (4, 12, 1), (3, 12, 13), (7, 14, 8), (0, 0, 1), (1, 14, 15), (2, 8, 0), (2, 9, 0), (0, 12, 1), (2, 13, 12), (1, 2, 9), (4, 15, 8), (3, 9, 0), (6, 3, 9), (5, 2), (1, 13, 12), (3, 14, 8), (7, 9, 0), (4, 3, 9), (7, 15, 14), (0, 8, 0), (4, 13, 12), (4, 2, 9), (2, 14, 8), (0, 9, 0), (2, 3, 9), (5, 15, 8), (4, 14, 15), (5, 3), (0, 13, 12), (2, 2, 9), (6, 2, 8), (3, 3, 9), (3, 15, 14), (5, 0), (3, 2, 9), (0, 15, 8), (0, 2, 8), (7, 3, 9), (2, 15, 14), (3, 0), (7, 2, 9), (0, 3, 9), (5, 14, 15), (2, 0), (6, 5), (0, 14, 15))
-LATE = ((6, 2), (6, 0), (6, 4), (5, 4), (4, 3), (4, 2), (4, 0), (7, 6), (7, 4), (7, 2), (7, 0), (7, 1), (5, 1), (3, 1), (2, 1))
-RETURNS = ((2, 14, 15), (2, 2, 8), (2, 3, 9), (2, 15, 8), (3, 14, 15), (3, 2, 9), (3, 3, 9), (3, 15, 8), (1, 14, 15), (0, 2, 8), (1, 2, 9), (1, 3, 9), (1, 15, 8), (0, 14, 15), (2, 8, 0), (2, 9, 0), (0, 3, 9), (0, 15, 8), (3, 8, 0), (3, 9, 0), (1, 8, 0), (1, 9, 0), (2, 13, 12), (2, 0, 1), (2, 12, 1), (0, 8, 0), (0, 9, 0), (3, 12, 13), (3, 0, 1), (3, 13, 1), (1, 13, 12), (1, 0, 1), (1, 12, 1), (0, 13, 12), (2, 1, 10), (0, 0, 1), (0, 12, 1), (3, 1, 10), (1, 1, 10), (0, 4, 6), (2, 11, 7), (0, 6, 5), (2, 7, 5), (2, 10, 5), (0, 1, 10), (1, 7, 11), (3, 6, 4), (1, 11, 5), (3, 4, 5), (3, 10, 5), (0, 11, 7), (1, 4, 6), (0, 7, 5), (1, 6, 5), (1, 10, 5), (2, 4, 6), (3, 11, 7), (0, 10, 5), (2, 6, 5), (3, 7, 5))
+HELD = (35, 33, 73, 9, 69, 5, 80, 48, 3, 65, 64, 32, 13, 77, 113, 19)
+STEPS = ((2, 6, 10), (2, 8, 10), (4, 9, 10), (6, 7, 10), (1, 7, 10), (1, 8, 10), (7, 6, 10), (7, 9, 10), (2, 9, 10), (3, 6, 10), (3, 7, 10), (3, 8, 10), (6, 9, 10), (7, 8, 10), (4, 5, 9), (4, 12, 9), (2, 11, 6), (6, 11, 7), (1, 9, 10), (6, 8, 10), (7, 5, 9), (7, 12, 9), (1, 11, 7), (7, 11, 6), (0, 9, 10), (4, 6, 10), (5, 8, 10), (7, 14, 9), (2, 4, 9), (2, 12, 9), (4, 4, 5), (4, 13, 12), (1, 15, 8), (3, 9, 10), (4, 8, 10), (5, 7, 10), (6, 4, 9), (6, 13, 9), (7, 4, 5), (7, 13, 12), (0, 8, 10), (2, 14, 9), (3, 11, 6), (5, 9, 10), (1, 4, 9), (1, 12, 9), (2, 5, 4), (2, 13, 12), (0, 7, 10), (1, 14, 7), (0, 5, 9), (0, 13, 9), (4, 11, 6), (4, 15, 6), (6, 5, 4), (6, 12, 13), (5, 15, 8), (6, 1, 11), (7, 0, 11), (3, 5, 9), (3, 12, 9), (5, 11, 7), (1, 5, 4), (1, 13, 12), (3, 14, 7), (4, 14, 9), (6, 15, 8), (5, 5, 9), (5, 12, 9), (3, 0, 11), (1, 2, 12), (2, 3, 5), (0, 4, 5), (0, 12, 13), (4, 4), (0, 15, 8), (2, 15, 6), (0, 11, 7), (0, 14, 7), (4, 2, 13), (7, 3, 4), (3, 4, 5), (3, 13, 12), (1, 0, 15), (1, 1, 14), (3, 15, 6), (5, 14, 7), (0, 2, 13), (3, 2, 4), (5, 4, 5), (5, 13, 12), (2, 1, 14), (4, 0, 11), (6, 14, 7), (7, 15, 8), (5, 3, 13), (6, 3, 4), (1, 3, 2), (2, 2, 3), (6, 6), (1, 6, 15), (6, 6, 11), (7, 7, 11), (0, 0, 11), (4, 3, 2), (7, 2, 3), (6, 4), (2, 7, 14), (3, 1, 14), (5, 0, 15), (5, 1, 11), (0, 3, 2), (3, 3, 2), (6, 5), (0, 1, 11), (2, 0, 15), (4, 7, 14), (5, 6, 11), (5, 2, 3), (6, 2, 3), (5, 4), (0, 6, 10), (4, 1, 14), (6, 0, 11), (7, 1, 11))
+LATE = ((5, 2), (7, 6), (7, 5), (7, 2), (7, 1), (5, 1), (4, 1), (7, 0), (6, 3), (6, 0), (4, 0), (3, 2), (3, 1), (1, 0), (0, 0))
+RETURNS = ((1, 2, 3), (0, 14, 1), (1, 3, 5), (3, 2, 3), (1, 0, 11), (1, 1, 11), (3, 1, 14), (3, 3, 12), (0, 2, 3), (2, 3, 2), (1, 15, 6), (2, 1, 11), (2, 7, 10), (3, 0, 15), (0, 3, 5), (2, 2, 13), (1, 4, 5), (1, 12, 13), (0, 0, 11), (0, 1, 11), (2, 0, 15), (2, 14, 9), (1, 5, 9), (1, 13, 9), (3, 5, 4), (3, 13, 12), (0, 15, 8), (1, 8, 10), (1, 11, 7), (1, 14, 7), (3, 4, 9), (3, 12, 9), (0, 4, 5), (0, 12, 13), (0, 6, 10), (3, 11, 7), (3, 14, 7), (3, 15, 6), (0, 5, 9), (0, 13, 9), (2, 5, 4), (2, 13, 12), (0, 11, 7), (1, 9, 10), (2, 11, 6), (2, 15, 6), (2, 4, 9), (2, 12, 9), (1, 6, 10), (1, 7, 10), (2, 8, 10), (3, 9, 10), (0, 9, 10), (3, 6, 10), (3, 7, 10), (3, 8, 10), (0, 7, 10), (0, 8, 10), (2, 6, 10), (2, 9, 10))
 N = len(HELD)
 ROWS = 128
 TASKS = tuple(s for s in STEPS if len(s) == 2) + LATE

time: 81.7 us -> 65.4 us (0.80)
  Pallas kernels: 79.6 us -> 63.3 us
    pallas_call x1, Pallas kernels: 79.6 us -> 63.3 us  [local(): pl.pallas_call(kernel, out_shape=jax.ShapeDtypeStruct((ROWS, D), F32), in...]
where the time goes in v3:
time: 65.4 us; the launch traced here: 65.2 us
  Pallas kernels  63.3 us (97%)
  local copies, waits for them, and re-layouts  1.89 us (3%)
    pallas_call x1, Pallas kernels, local(): pl.pallas_call(kernel, out_shape=jax.ShapeDtypeStruct((ROWS, D), F32), in...  63.3 us
    unnamed x1, local copies, waits for them, and re-layouts  1.89 us

profile of v3, /device:TPU:1, one launch (start us, length us, event | category | flops | bytes accessed | tf_op | source)
XLA Modules:
  0.0 65.2 jit_solution(8003989443317681009)
XLA Ops:
  0.0 63.3 %relational_grad.1 = f32[128,1024]{1,0:T(8,128)} custom-call(bf16[128,1024]{1,0:T(8,128)(2,1)} %student_ref.1, bf16[128,1024]{1,0:T(8,128)(2,1)} %teacher_ref.1), custom_call_target="tpu_custom_call" | custom-call | tf_op jit(solution)/shard_map/relational_grad/pallas_call | solution.py:194
  63.3 1.9 %copy.4 = f32[128,1024]{1,0:T(8,128)} copy(f32[128,1024]{1,0:T(8,128)} %relational_grad.1) | data formatting | bytes 1048576

commit v4 on v3

--- a/solution.py
+++ b/solution.py
@@ -10,14 +10,13 @@
 BF16 = jnp.bfloat16
 MESH = pl.DeviceIdType.MESH
 
-HELD = (35, 33, 73, 9, 69, 5, 80, 48, 3, 65, 64, 32, 13, 77, 113, 19)
-STEPS = ((2, 6, 10), (2, 8, 10), (4, 9, 10), (6, 7, 10), (1, 7, 10), (1, 8, 10), (7, 6, 10), (7, 9, 10), (2, 9, 10), (3, 6, 10), (3, 7, 10), (3, 8, 10), (6, 9, 10), (7, 8, 10), (4, 5, 9), (4, 12, 9), (2, 11, 6), (6, 11, 7), (1, 9, 10), (6, 8, 10), (7, 5, 9), (7, 12, 9), (1, 11, 7), (7, 11, 6), (0, 9, 10), (4, 6, 10), (5, 8, 10), (7, 14, 9), (2, 4, 9), (2, 12, 9), (4, 4, 5), (4, 13, 12), (1, 15, 8), (3, 9, 10), (4, 8, 10), (5, 7, 10), (6, 4, 9), (6, 13, 9), (7, 4, 5), (7, 13, 12), (0, 8, 10), (2, 14, 9), (3, 11, 6), (5, 9, 10), (1, 4, 9), (1, 12, 9), (2, 5, 4), (2, 13, 12), (0, 7, 10), (1, 14, 7), (0, 5, 9), (0, 13, 9), (4, 11, 6), (4, 15, 6), (6, 5, 4), (6, 12, 13), (5, 15, 8), (6, 1, 11), (7, 0, 11), (3, 5, 9), (3, 12, 9), (5, 11, 7), (1, 5, 4), (1, 13, 12), (3, 14, 7), (4, 14, 9), (6, 15, 8), (5, 5, 9), (5, 12, 9), (3, 0, 11), (1, 2, 12), (2, 3, 5), (0, 4, 5), (0, 12, 13), (4, 4), (0, 15, 8), (2, 15, 6), (0, 11, 7), (0, 14, 7), (4, 2, 13), (7, 3, 4), (3, 4, 5), (3, 13, 12), (1, 0, 15), (1, 1, 14), (3, 15, 6), (5, 14, 7), (0, 2, 13), (3, 2, 4), (5, 4, 5), (5, 13, 12), (2, 1, 14), (4, 0, 11), (6, 14, 7), (7, 15, 8), (5, 3, 13), (6, 3, 4), (1, 3, 2), (2, 2, 3), (6, 6), (1, 6, 15), (6, 6, 11), (7, 7, 11), (0, 0, 11), (4, 3, 2), (7, 2, 3), (6, 4), (2, 7, 14), (3, 1, 14), (5, 0, 15), (5, 1, 11), (0, 3, 2), (3, 3, 2), (6, 5), (0, 1, 11), (2, 0, 15), (4, 7, 14), (5, 6, 11), (5, 2, 3), (6, 2, 3), (5, 4), (0, 6, 10), (4, 1, 14), (6, 0, 11), (7, 1, 11))
-LATE = ((5, 2), (7, 6), (7, 5), (7, 2), (7, 1), (5, 1), (4, 1), (7, 0), (6, 3), (6, 0), (4, 0), (3, 2), (3, 1), (1, 0), (0, 0))
-RETURNS = ((1, 2, 3), (0, 14, 1), (1, 3, 5), (3, 2, 3), (1, 0, 11), (1, 1, 11), (3, 1, 14), (3, 3, 12), (0, 2, 3), (2, 3, 2), (1, 15, 6), (2, 1, 11), (2, 7, 10), (3, 0, 15), (0, 3, 5), (2, 2, 13), (1, 4, 5), (1, 12, 13), (0, 0, 11), (0, 1, 11), (2, 0, 15), (2, 14, 9), (1, 5, 9), (1, 13, 9), (3, 5, 4), (3, 13, 12), (0, 15, 8), (1, 8, 10), (1, 11, 7), (1, 14, 7), (3, 4, 9), (3, 12, 9), (0, 4, 5), (0, 12, 13), (0, 6, 10), (3, 11, 7), (3, 14, 7), (3, 15, 6), (0, 5, 9), (0, 13, 9), (2, 5, 4), (2, 13, 12), (0, 11, 7), (1, 9, 10), (2, 11, 6), (2, 15, 6), (2, 4, 9), (2, 12, 9), (1, 6, 10), (1, 7, 10), (2, 8, 10), (3, 9, 10), (0, 9, 10), (3, 6, 10), (3, 7, 10), (3, 8, 10), (0, 7, 10), (0, 8, 10), (2, 6, 10), (2, 9, 10))
+HELD = (112, 19, 67, 64, 69, 113, 1, 13, 5, 77, 32, 80, 9, 73, 33, 35)
+STEPS = ((0, 0, 2, 3), (0, 1, 6, 3), (0, 1, 0, 3), (0, 3, 11, 3), (0, 0, 6, 3), (0, 0, 0, 3), (0, 1, 2, 3), (0, 1, 11, 3), (0, 2, 6, 3), (0, 2, 11, 3), (0, 3, 2, 3), (0, 3, 0, 3), (0, 1, 4, 6), (0, 1, 9, 6), (0, 0, 11, 3), (0, 2, 2, 3), (0, 2, 0, 3), (0, 3, 6, 3), (0, 0, 7, 6), (0, 0, 4, 6), (0, 1, 8, 4), (0, 1, 7, 9), (0, 1, 1, 11), (0, 1, 10, 0), (0, 2, 7, 6), (0, 2, 4, 6), (0, 2, 10, 11), (0, 3, 5, 0), (0, 0, 8, 4), (0, 0, 9, 7), (0, 0, 10, 0), (0, 3, 1, 11), (0, 3, 10, 11), (0, 3, 8, 6), (0, 3, 7, 6), (0, 2, 5, 0), (0, 0, 12, 4), (0, 2, 8, 4), (0, 2, 9, 7), (0, 2, 12, 7), (0, 0, 1, 2), (0, 0, 5, 0), (0, 1, 5, 6), (0, 2, 1, 11), (0, 1, 12, 7), (0, 3, 4, 8), (0, 3, 9, 7), (0, 3, 12, 8), (1, 3, 1), (0, 0, 14, 10), (0, 0, 15, 10), (0, 2, 14, 5), (0, 3, 15, 1), (1, 5, 3), (1, 5, 4), (1, 5, 1), (0, 0, 13, 12), (0, 2, 13, 12), (0, 1, 15, 1), (0, 2, 15, 10), (0, 3, 14, 10), (1, 4, 1), (0, 1, 14, 5), (1, 2, 0), (1, 2, 1), (1, 2, 2), (0, 1, 13, 12), (0, 3, 13, 12), (1, 3, 0), (1, 3, 2), (1, 6, 0), (1, 6, 1), (2, 3, 2, 3), (2, 2, 2, 3), (2, 1, 2, 3), (1, 6, 2), (1, 7, 6), (1, 6, 5), (2, 2, 12, 13), (2, 1, 13, 12), (2, 0, 13, 12), (2, 3, 13, 12), (1, 7, 2), (1, 7, 3), (2, 2, 13, 8), (2, 1, 12, 9), (2, 0, 12, 8), (2, 3, 12, 9), (2, 2, 7, 9), (2, 1, 7, 9), (1, 7, 7), (2, 0, 15, 1), (2, 0, 14, 5), (2, 2, 15, 10), (2, 3, 14, 10), (2, 3, 15, 1), (2, 1, 14, 10), (2, 1, 15, 10), (2, 2, 14, 5), (1, 4, 2), (1, 5, 2), (2, 2, 4, 8), (2, 0, 10, 11), (2, 3, 5, 0), (2, 1, 4, 8), (2, 1, 5, 0), (2, 0, 4, 8), (2, 3, 4, 8), (1, 4, 0), (2, 0, 0, 3), (2, 2, 1, 11), (2, 2, 8, 6), (2, 2, 9, 6), (2, 0, 1, 2), (2, 1, 8, 6), (2, 1, 9, 6), (2, 3, 10, 0), (2, 0, 9, 7), (2, 0, 5, 6), (2, 1, 1, 11), (2, 2, 10, 11), (2, 0, 8, 6), (2, 3, 9, 7), (2, 3, 8, 6), (2, 3, 1, 11), (2, 2, 5, 0), (2, 0, 7, 6), (2, 1, 10, 0), (2, 3, 7, 6), (2, 0, 11, 3), (2, 2, 6, 3), (2, 0, 2, 3), (2, 3, 0, 3), (2, 1, 11, 3), (2, 1, 6, 3), (2, 2, 11, 3), (2, 2, 0, 3), (2, 3, 11, 3), (2, 0, 6, 3), (2, 1, 0, 3), (2, 3, 6, 3))
+
+
 N = len(HELD)
 ROWS = 128
-TASKS = tuple(s for s in STEPS if len(s) == 2) + LATE
-SENDS = tuple(s for s in STEPS if len(s) == 3)
+SENDS, TASKS, RETURNS = (tuple(s[1:] for s in STEPS if s[0] == kind) for kind in range(3))
 OWN = ({i for _, _, i in SENDS} - {j for _, j, _ in SENDS}).pop()
 PIECES = 1 + max(h for h, _, _ in SENDS)
 PARTS = 1 + max(h for h, _, _ in RETURNS)
@@ -95,7 +94,7 @@
             gathers[h, j].wait_recv()
             arrived.add((h, j))
 
-    tasks = list(zip(TASKS, weights()))
+    weight_of = dict(zip(TASKS, weights()))
     fresh = set(range(N // 2))
 
     def add(g, value):
@@ -109,8 +108,8 @@
     def dot(a, b, dims):
         return lax.dot_general(a, b, (dims, ((), ())), preferred_element_type=F32)
 
-    def run(task):
-        (g, h), quad = task
+    def run(g, h):
+        quad = weight_of[g, h]
         for b in (2 * g, 2 * g + 1, 2 * h, 2 * h + 1):
             for piece in range(PIECES):
                 await_piece(piece, b)
@@ -135,11 +134,7 @@
         if g != h:
             add(h, dot(mismatch, s_g, ((0,), (0,))))
 
-    for step in STEPS:
-        if len(step) == 2:
-            run(tasks.pop(0))
-            continue
-        h, j, i = step
+    def send(h, j, i):
         await_piece(h, i)
         gathers[h, j] = pltpu.make_async_remote_copy(
             src_ref=held.at[i, rows_of(h), :],
@@ -152,17 +147,14 @@
         gathers[h, j].start()
 
     def total(h, j):
-        for task in [k for k in tasks if j // 2 in k[0]]:
-            run(task)
-            tasks.remove(task)
         value = pull[j, part_of(h), :]
-        for part, child, parent in RETURNS:
-            if (part, parent) == (h, j):
+        for part, child, goal in RETURNS:
+            if (part, goal) == (h, j):
                 returns[h, child].wait_recv()
                 value += come[child, part_of(h), :].astype(F32)
         return value
 
-    for h, j, i in RETURNS:
+    def give_back(h, j, i):
         sent[j, part_of(h), :] = total(h, j).astype(BF16)
         returns[h, j] = pltpu.make_async_remote_copy(
             src_ref=sent.at[j, part_of(h), :],
@@ -173,6 +165,9 @@
             device_id_type=MESH,
         )
         returns[h, j].start()
+
+    for step in STEPS:
+        (send, run, give_back)[step[0]](*step[1:])
 
     scale = 12.0 * (D / (ROWS * 128)) ** 0.5
     for h in range(PARTS):

time: 65.4 us -> 62.5 us (0.956)
  Pallas kernels: 63.3 us -> 60.5 us
    pallas_call x1, Pallas kernels: 63.3 us -> 60.5 us  [local(): pl.pallas_call(kernel, out_shape=jax.ShapeDtypeStruct((ROWS, D), F32), in...]
where the time goes in v4:
time: 62.5 us; the launch traced here: 62.4 us
  Pallas kernels  60.5 us (97%)
  local copies, waits for them, and re-layouts  1.89 us (3%)
    pallas_call x1, Pallas kernels, local(): pl.pallas_call(kernel, out_shape=jax.ShapeDtypeStruct((ROWS, D), F32), in...  60.5 us
    unnamed x1, local copies, waits for them, and re-layouts  1.89 us

profile of v4, /device:TPU:1, one launch (start us, length us, event | category | flops | bytes accessed | tf_op | source)
XLA Modules:
  0.0 62.4 jit_solution(2664611697053512052)
XLA Ops:
  0.0 60.5 %relational_grad.1 = f32[128,1024]{1,0:T(8,128)} custom-call(bf16[128,1024]{1,0:T(8,128)(2,1)} %student_ref.1, bf16[128,1024]{1,0:T(8,128)(2,1)} %teacher_ref.1), custom_call_target="tpu_custom_call" | custom-call | tf_op jit(solution)/shard_map/relational_grad/pallas_call | solution.py:189
  60.5 1.9 %copy.4 = f32[128,1024]{1,0:T(8,128)} copy(f32[128,1024]{1,0:T(8,128)} %relational_grad.1) | data formatting | bytes 1048576

commit v5 on v4

--- a/solution.py
+++ b/solution.py
@@ -53,7 +53,10 @@
     return out
 
 
-def kernel(student_ref, teacher_ref, out_ref, held, pull, sent, come, g_send, g_recv, r_send, r_recv):
+def kernel(
+    student_hbm, teacher_hbm, out_hbm, student_ref, teacher_ref, out_ref, held, pull, sent, come,
+    in_sem, out_sem, g_send, g_recv, r_send, r_recv,
+):
     gr, gc = lax.axis_index("gr"), lax.axis_index("gc")
     place = (lax.rem(gc // 2, 4), (gr // 4) * 2 + gc // 8, lax.rem(gr, 4), lax.rem(gc, 2))
 
@@ -69,6 +72,15 @@
     barrier = pltpu.get_barrier_semaphore()
     for step in target:
         pl.semaphore_signal(barrier, inc=1, device_id=target[step], device_id_type=MESH)
+
+    loads = [
+        pltpu.make_async_copy(student_hbm, student_ref, in_sem.at[0]),
+        pltpu.make_async_copy(teacher_hbm, teacher_ref, in_sem.at[1]),
+    ]
+    for load in loads:
+        load.start()
+    for load in loads:
+        load.wait()
 
     def unit(ref, rows):
         values = ref[rows, :].astype(F32)
@@ -169,6 +181,7 @@
     for step in STEPS:
         (send, run, give_back)[step[0]](*step[1:])
 
+    stores = []
     scale = 12.0 * (D / (ROWS * 128)) ** 0.5
     for h in range(PARTS):
         value = total(h, OWN)
@@ -176,26 +189,37 @@
         inverse = unit(student_ref, part_of(h))[1]
         radial = jnp.sum(unit_float * value, axis=-1, keepdims=True)
         out_ref[part_of(h), :] = scale * inverse * (value - radial * unit_float)
+        stores.append(
+            pltpu.make_async_copy(out_ref.at[part_of(h), :], out_hbm.at[part_of(h), :], out_sem.at[h])
+        )
+        stores[-1].start()
     for h, j, _ in SENDS:
         gathers[h, j].wait_send()
     for h, j, _ in RETURNS:
         returns[h, j].wait_send()
+    for store in stores:
+        store.wait()
 
 
 def local(student, teacher):
-    vmem = pl.BlockSpec(memory_space=pltpu.VMEM)
+    hbm = pl.BlockSpec(memory_space=pl.ANY)
     g_sems = pltpu.SemaphoreType.DMA((PIECES, N))
     r_sems = pltpu.SemaphoreType.DMA((PARTS, N))
     return pl.pallas_call(
         kernel,
         out_shape=jax.ShapeDtypeStruct((ROWS, D), F32),
-        in_specs=[vmem, vmem],
-        out_specs=vmem,
+        in_specs=[hbm, hbm],
+        out_specs=hbm,
         scratch_shapes=[
+            pltpu.VMEM((ROWS, D), BF16),
+            pltpu.VMEM((ROWS, D), BF16),
+            pltpu.VMEM((ROWS, D), F32),
             pltpu.VMEM((N, ROWS, 2 * D), BF16),
             pltpu.VMEM((N, ROWS, D), F32),
             pltpu.VMEM((N, ROWS, D), BF16),
             pltpu.VMEM((N, ROWS, D), BF16),
+            pltpu.SemaphoreType.DMA((2,)),
+            pltpu.SemaphoreType.DMA((PARTS,)),
             g_sems,
             g_sems,
             r_sems,

time: 62.5 us -> 61.2 us (0.979)
  Pallas kernels: 60.5 us -> 59.2 us
    pallas_call x1, Pallas kernels: 60.5 us -> 59.2 us  [local(): pl.pallas_call(kernel, out_shape=jax.ShapeDtypeStruct((ROWS, D), F32), in...]
where the time goes in v5:
time: 61.2 us; the launch traced here: 61.1 us
  Pallas kernels  59.2 us (97%)
  local copies, waits for them, and re-layouts  1.89 us (3%)
    pallas_call x1, Pallas kernels, local(): pl.pallas_call(kernel, out_shape=jax.ShapeDtypeStruct((ROWS, D), F32), in...  59.2 us
    unnamed x1, local copies, waits for them, and re-layouts  1.89 us

profile of v5, /device:TPU:1, one launch (start us, length us, event | category | flops | bytes accessed | tf_op | source)
XLA Modules:
  0.0 61.1 jit_solution(5379154032781350420)
XLA Ops:
  0.0 59.2 %relational_grad.1 = f32[128,1024]{1,0:T(8,128)} custom-call(bf16[128,1024]{1,0:T(8,128)(2,1)} %student_hbm.1, bf16[128,1024]{1,0:T(8,128)(2,1)} %teacher_hbm.1), custom_call_target="tpu_custom_call" | custom-call | tf_op jit(solution)/shard_map/relational_grad/pallas_call | solution.py:208
  59.2 1.9 %copy.4 = f32[128,1024]{1,0:T(8,128)} copy(f32[128,1024]{1,0:T(8,128)} %relational_grad.1) | data formatting | bytes 1048576

commit v6 on v5

--- a/solution.py
+++ b/solution.py
@@ -10,8 +10,8 @@
 BF16 = jnp.bfloat16
 MESH = pl.DeviceIdType.MESH
 
-HELD = (112, 19, 67, 64, 69, 113, 1, 13, 5, 77, 32, 80, 9, 73, 33, 35)
-STEPS = ((0, 0, 2, 3), (0, 1, 6, 3), (0, 1, 0, 3), (0, 3, 11, 3), (0, 0, 6, 3), (0, 0, 0, 3), (0, 1, 2, 3), (0, 1, 11, 3), (0, 2, 6, 3), (0, 2, 11, 3), (0, 3, 2, 3), (0, 3, 0, 3), (0, 1, 4, 6), (0, 1, 9, 6), (0, 0, 11, 3), (0, 2, 2, 3), (0, 2, 0, 3), (0, 3, 6, 3), (0, 0, 7, 6), (0, 0, 4, 6), (0, 1, 8, 4), (0, 1, 7, 9), (0, 1, 1, 11), (0, 1, 10, 0), (0, 2, 7, 6), (0, 2, 4, 6), (0, 2, 10, 11), (0, 3, 5, 0), (0, 0, 8, 4), (0, 0, 9, 7), (0, 0, 10, 0), (0, 3, 1, 11), (0, 3, 10, 11), (0, 3, 8, 6), (0, 3, 7, 6), (0, 2, 5, 0), (0, 0, 12, 4), (0, 2, 8, 4), (0, 2, 9, 7), (0, 2, 12, 7), (0, 0, 1, 2), (0, 0, 5, 0), (0, 1, 5, 6), (0, 2, 1, 11), (0, 1, 12, 7), (0, 3, 4, 8), (0, 3, 9, 7), (0, 3, 12, 8), (1, 3, 1), (0, 0, 14, 10), (0, 0, 15, 10), (0, 2, 14, 5), (0, 3, 15, 1), (1, 5, 3), (1, 5, 4), (1, 5, 1), (0, 0, 13, 12), (0, 2, 13, 12), (0, 1, 15, 1), (0, 2, 15, 10), (0, 3, 14, 10), (1, 4, 1), (0, 1, 14, 5), (1, 2, 0), (1, 2, 1), (1, 2, 2), (0, 1, 13, 12), (0, 3, 13, 12), (1, 3, 0), (1, 3, 2), (1, 6, 0), (1, 6, 1), (2, 3, 2, 3), (2, 2, 2, 3), (2, 1, 2, 3), (1, 6, 2), (1, 7, 6), (1, 6, 5), (2, 2, 12, 13), (2, 1, 13, 12), (2, 0, 13, 12), (2, 3, 13, 12), (1, 7, 2), (1, 7, 3), (2, 2, 13, 8), (2, 1, 12, 9), (2, 0, 12, 8), (2, 3, 12, 9), (2, 2, 7, 9), (2, 1, 7, 9), (1, 7, 7), (2, 0, 15, 1), (2, 0, 14, 5), (2, 2, 15, 10), (2, 3, 14, 10), (2, 3, 15, 1), (2, 1, 14, 10), (2, 1, 15, 10), (2, 2, 14, 5), (1, 4, 2), (1, 5, 2), (2, 2, 4, 8), (2, 0, 10, 11), (2, 3, 5, 0), (2, 1, 4, 8), (2, 1, 5, 0), (2, 0, 4, 8), (2, 3, 4, 8), (1, 4, 0), (2, 0, 0, 3), (2, 2, 1, 11), (2, 2, 8, 6), (2, 2, 9, 6), (2, 0, 1, 2), (2, 1, 8, 6), (2, 1, 9, 6), (2, 3, 10, 0), (2, 0, 9, 7), (2, 0, 5, 6), (2, 1, 1, 11), (2, 2, 10, 11), (2, 0, 8, 6), (2, 3, 9, 7), (2, 3, 8, 6), (2, 3, 1, 11), (2, 2, 5, 0), (2, 0, 7, 6), (2, 1, 10, 0), (2, 3, 7, 6), (2, 0, 11, 3), (2, 2, 6, 3), (2, 0, 2, 3), (2, 3, 0, 3), (2, 1, 11, 3), (2, 1, 6, 3), (2, 2, 11, 3), (2, 2, 0, 3), (2, 3, 11, 3), (2, 0, 6, 3), (2, 1, 0, 3), (2, 3, 6, 3))
+HELD = (1, 3, 73, 9, 33, 99, 0, 49, 5, 69, 83, 32, 13, 77, 112, 16)
+STEPS = ((0, 0, 14, 6), (0, 2, 0, 6), (0, 2, 15, 6), (0, 3, 1, 6), (0, 1, 0, 6), (0, 2, 1, 6), (0, 2, 14, 6), (0, 3, 15, 6), (0, 0, 0, 6), (0, 0, 1, 6), (0, 0, 15, 6), (0, 1, 14, 6), (0, 2, 8, 0), (0, 2, 13, 0), (0, 1, 1, 6), (0, 1, 15, 6), (0, 3, 0, 6), (0, 3, 14, 6), (0, 1, 12, 0), (0, 1, 9, 0), (0, 2, 12, 13), (0, 2, 9, 8), (0, 0, 7, 14), (0, 2, 11, 14), (0, 3, 11, 15), (0, 3, 10, 15), (0, 0, 12, 0), (0, 0, 9, 0), (0, 1, 8, 9), (0, 1, 13, 12), (0, 0, 11, 14), (0, 2, 7, 14), (0, 3, 9, 0), (0, 3, 13, 0), (0, 1, 11, 15), (0, 1, 10, 15), (1, 7, 0), (1, 0, 0), (0, 1, 2, 12), (0, 2, 2, 9), (0, 0, 8, 9), (0, 0, 13, 12), (0, 0, 10, 1), (0, 1, 7, 0), (0, 2, 10, 15), (0, 3, 7, 14), (0, 0, 3, 8), (0, 3, 8, 9), (0, 3, 12, 13), (0, 3, 3, 13), (0, 3, 4, 11), (0, 3, 5, 10), (0, 1, 5, 11), (0, 2, 4, 7), (1, 7, 4), (1, 7, 6), (1, 6, 0), (0, 1, 3, 2), (0, 2, 3, 2), (0, 0, 4, 7), (0, 1, 4, 11), (0, 2, 5, 11), (1, 6, 6), (0, 0, 5, 10), (1, 7, 5), (1, 4, 3), (1, 5, 4), (0, 0, 2, 3), (0, 3, 2, 3), (2, 3, 9, 8), (2, 1, 9, 8), (2, 2, 8, 9), (2, 0, 9, 8), (1, 6, 3), (1, 1, 0), (2, 1, 8, 0), (2, 0, 8, 0), (1, 3, 1), (1, 5, 1), (1, 2, 1), (1, 7, 1), (2, 3, 3, 2), (2, 1, 2, 3), (2, 2, 14, 6), (2, 0, 2, 3), (2, 2, 3, 2), (2, 0, 15, 6), (2, 3, 15, 6), (1, 2, 0), (2, 3, 2, 8), (2, 1, 3, 13), (2, 0, 3, 13), (2, 2, 2, 9), (1, 2, 2), (1, 3, 2), (1, 6, 2), (2, 3, 5, 10), (2, 1, 4, 11), (2, 1, 5, 11), (2, 0, 4, 11), (2, 2, 5, 11), (2, 3, 4, 7), (2, 0, 5, 11), (2, 2, 4, 11), (1, 6, 5), (2, 3, 12, 13), (2, 3, 11, 14), (2, 3, 8, 0), (2, 1, 12, 13), (2, 2, 13, 12), (2, 0, 10, 1), (2, 1, 10, 15), (2, 2, 10, 15), (1, 3, 0), (2, 3, 13, 0), (2, 1, 7, 14), (2, 2, 1, 6), (2, 2, 7, 0), (2, 1, 13, 0), (2, 0, 7, 0), (2, 2, 12, 0), (2, 2, 9, 0), (2, 3, 10, 1), (2, 0, 13, 12), (2, 1, 11, 15), (2, 1, 1, 6), (2, 3, 7, 14), (2, 0, 12, 0), (2, 0, 1, 6), (2, 2, 11, 15), (2, 0, 11, 14), (2, 3, 0, 6), (2, 3, 1, 6), (2, 1, 0, 6), (2, 1, 14, 6), (2, 1, 15, 6), (2, 2, 0, 6), (2, 3, 14, 6), (2, 2, 15, 6), (2, 0, 14, 6), (2, 0, 0, 6))
 
 
 N = len(HELD)
@@ -54,7 +54,7 @@
 
 
 def kernel(
-    student_hbm, teacher_hbm, out_hbm, student_ref, teacher_ref, out_ref, held, pull, sent, come,
+    student_hbm, teacher_hbm, out_hbm, student_ref, teacher_ref, out_ref, inverse_ref, held, pull, sent, come,
     in_sem, out_sem, g_send, g_recv, r_send, r_recv,
 ):
     gr, gc = lax.axis_index("gr"), lax.axis_index("gc")
@@ -94,7 +94,8 @@
         return pl.ds(h * (ROWS // PARTS), ROWS // PARTS)
 
     for h in range(PIECES):
-        held[OWN, rows_of(h), 0:D] = unit(student_ref, rows_of(h))[0]
+        held[OWN, rows_of(h), 0:D], inverse = unit(student_ref, rows_of(h))
+        inverse_ref[rows_of(h), :] = jnp.broadcast_to(inverse, (ROWS // PIECES, 128))
         held[OWN, rows_of(h), D : 2 * D] = unit(teacher_ref, rows_of(h))[0]
     pl.semaphore_wait(barrier, len(target))
 
@@ -178,24 +179,29 @@
         )
         returns[h, j].start()
 
-    for step in STEPS:
+    last_task = max(n for n, step in enumerate(STEPS) if step[0] == 1)
+    for n, step in enumerate(STEPS):
         (send, run, give_back)[step[0]](*step[1:])
-
+        if n == last_task:
+            for h, j, _ in SENDS:
+                gathers[h, j].wait_send()
+
+    for h, j, _ in RETURNS[:-N]:
+        returns[h, j].wait_send()
     stores = []
     scale = 12.0 * (D / (ROWS * 128)) ** 0.5
-    for h in range(PARTS):
+    final = {h: n for n, (h, _, i) in enumerate(RETURNS) if i == OWN}
+    for h in sorted(final, key=final.get):
         value = total(h, OWN)
         unit_float = held[OWN, part_of(h), 0:D].astype(F32)
-        inverse = unit(student_ref, part_of(h))[1]
+        inverse = inverse_ref[part_of(h), 0:1]
         radial = jnp.sum(unit_float * value, axis=-1, keepdims=True)
         out_ref[part_of(h), :] = scale * inverse * (value - radial * unit_float)
         stores.append(
             pltpu.make_async_copy(out_ref.at[part_of(h), :], out_hbm.at[part_of(h), :], out_sem.at[h])
         )
         stores[-1].start()
-    for h, j, _ in SENDS:
-        gathers[h, j].wait_send()
-    for h, j, _ in RETURNS:
+    for h, j, _ in RETURNS[-N:]:
         returns[h, j].wait_send()
     for store in stores:
         store.wait()
@@ -214,6 +220,7 @@
             pltpu.VMEM((ROWS, D), BF16),
             pltpu.VMEM((ROWS, D), BF16),
             pltpu.VMEM((ROWS, D), F32),
+            pltpu.VMEM((ROWS, 128), F32),
             pltpu.VMEM((N, ROWS, 2 * D), BF16),
             pltpu.VMEM((N, ROWS, D), F32),
             pltpu.VMEM((N, ROWS, D), BF16),

time: 61.2 us -> 60.8 us (level)
  no operation moved by 1% of the time
where the time goes in v6:
time: 60.8 us; the launch traced here: 60.6 us
  Pallas kernels  58.7 us (97%)
  local copies, waits for them, and re-layouts  1.89 us (3%)
    pallas_call x1, Pallas kernels, local(): pl.pallas_call(kernel, out_shape=jax.ShapeDtypeStruct((ROWS, D), F32), in...  58.7 us
    unnamed x1, local copies, waits for them, and re-layouts  1.89 us

profile of v6, /device:TPU:1, one launch (start us, length us, event | category | flops | bytes accessed | tf_op | source)
XLA Modules:
  0.0 60.6 jit_solution(16096296016528266926)
XLA Ops:
  0.0 58.7 %relational_grad.1 = f32[128,1024]{1,0:T(8,128)} custom-call(bf16[128,1024]{1,0:T(8,128)(2,1)} %student_hbm.1, bf16[128,1024]{1,0:T(8,128)(2,1)} %teacher_hbm.1), custom_call_target="tpu_custom_call" | custom-call | tf_op jit(solution)/shard_map/relational_grad/pallas_call | solution.py:214
  58.7 1.9 %copy.4 = f32[128,1024]{1,0:T(8,128)} copy(f32[128,1024]{1,0:T(8,128)} %relational_grad.1) | data formatting | bytes 1048576

commit v7 on v6

--- a/solution.py
+++ b/solution.py
@@ -207,11 +207,15 @@
         store.wait()
 
 
+def hand_on(in_ref, out_ref):
+    out_ref[...] = in_ref[...]
+
+
 def local(student, teacher):
     hbm = pl.BlockSpec(memory_space=pl.ANY)
     g_sems = pltpu.SemaphoreType.DMA((PIECES, N))
     r_sems = pltpu.SemaphoreType.DMA((PARTS, N))
-    return pl.pallas_call(
+    result = pl.pallas_call(
         kernel,
         out_shape=jax.ShapeDtypeStruct((ROWS, D), F32),
         in_specs=[hbm, hbm],
@@ -237,6 +241,14 @@
         ),
         name="relational_grad",
     )(student, teacher)
+    vmem = pl.BlockSpec(memory_space=pltpu.VMEM)
+    return pl.pallas_call(
+        hand_on,
+        out_shape=jax.ShapeDtypeStruct((ROWS, D), F32),
+        in_specs=[vmem],
+        out_specs=vmem,
+        name="hand_on",
+    )(result)
 
 
 def solution(mesh):

time: 60.8 us -> 60.8 us (level)
  Pallas kernels: 58.7 us -> 60.6 us
  local copies, waits for them, and re-layouts: 1.89 us -> 0 us
    unnamed x1 -> x0, local copies, waits for them, and re-layouts: 1.89 us -> none
    pallas_call x0 -> x1, Pallas kernels: none -> 1.87 us  [local(): pl.pallas_call(hand_on, out_shape=jax.ShapeDtypeStruct((ROWS, D), F32), i...]
where the time goes in v7:
time: 60.8 us; the launch traced here: 60.6 us
  Pallas kernels  60.6 us (100%)
    pallas_call x1, Pallas kernels, local(): pl.pallas_call(kernel, out_shape=jax.ShapeDtypeStruct((ROWS, D), F32), in...  58.7 us
    pallas_call x1, Pallas kernels, local(): pl.pallas_call(hand_on, out_shape=jax.ShapeDtypeStruct((ROWS, D), F32), i...  1.87 us

profile of v7, /device:TPU:1, one launch (start us, length us, event | category | flops | bytes accessed | tf_op | source)
XLA Modules:
  0.0 60.6 jit_solution(4528306413685924327)
XLA Ops:
  0.0 58.7 %relational_grad.1.in_ref = f32[128,1024]{1,0:T(8,128)} custom-call(bf16[128,1024]{1,0:T(8,128)(2,1)} %student_hbm.1, bf16[128,1024]{1,0:T(8,128)(2,1)} %teacher_hbm.1), custom_call_target="tpu_custom_call" | custom-call | tf_op jit(solution)/shard_map/relational_grad/pallas_call | solution.py:218
  58.7 1.9 %hand_on.1 = f32[128,1024]{1,0:T(8,128)} custom-call(f32[128,1024]{1,0:T(8,128)} %relational_grad.1.in_ref), custom_call_target="tpu_custom_call" | custom-call | tf_op jit(solution)/shard_map/hand_on/pallas_call | solution.py:245
